TPU v7x, 512 devices: a whole 4x8x8 slice. The times are simulated.
512 devices in a mesh: ctx: 64 (over z_lo, y, core), ch: 8 (over z_hi, x).
Axes of the slice: x: 4, y: 8, z: 8 (z_hi: 2, z_lo: 4; z = z_hi * 4 + z_lo), core: 2. Of those that a mesh axis runs over, the one named last changes fastest.
Arguments:
- projections: bfloat16 [3, 8192, 8192], P(None, 'ctx', 'ch'), may hold values from -150 to 150
- grouped_short_filters: float32 [3, 7, 512], P(None, None, 'ch'), may hold values from -2 to 2
- long_filter: float32 [8192, 8192], P('ctx', 'ch'), may hold values from 0 to 0.5
- norm_gain: float32 [8192], P('ch'), may hold values from 0.1 to 1.9
- out_grad: bfloat16 [8192, 8192], P('ctx', 'ch'), may hold values from -6 to 6
Outputs:
- output: bfloat16 [8192, 8192], P('ctx', 'ch')
- proj_grads: bfloat16 [3, 8192, 8192], P(None, 'ctx', 'ch')
- short_grads: float32 [3, 7, 512], P(None, None, 'ch')
- long_grad: float32 [8192, 8192], P('ctx', 'ch')
- gain_grad: float32 [8192], P('ch')
All inputs are finite; a program needn't handle non-finite values.
Results may differ from a plain program's by a relative error of at most 0.0064.
Values may be sent and summed in bfloat16 or wider, within the bound.
A program may use at most 64 MiB of HBM per device.

v0:
```python
import math

import jax
import jax.numpy as jnp
from jax import lax
from jax.sharding import PartitionSpec as P

D = 8192
GROUP = 16
KS = 7


epsilon = 1e-05


def passed_along(block, axis, distance):
    devices = range(lax.axis_size(axis))
    route = [(i - distance, i) for i in devices if i - distance in devices]
    return lax.ppermute(block, axis, route)


def contract(form, left, right):
    return jnp.einsum(form, left, right, precision=lax.Precision.HIGHEST)


def factor_sizes(period):
    inner_len = 1
    while 2 * inner_len * (2 * inner_len) <= period and period % (4 * inner_len) == 0:
        inner_len = inner_len * 2
    return (period // inner_len, inner_len)


def dft_tables(order):
    ordinal_list = jnp.arange(order, dtype=jnp.int32)
    phases = (ordinal_list[:, None] * ordinal_list[None, :] % order).astype(jnp.float32) * (
        2.0 * math.pi / order
    )
    return (jnp.cos(phases), jnp.sin(phases))


def make_tables(outer_len, inner_len):
    period = outer_len * inner_len
    cos_a, sin_a = dft_tables(outer_len)
    cos_b, sin_b = dft_tables(inner_len)
    row_ids = jnp.arange(outer_len, dtype=jnp.int32)[:, None]
    col_ids = jnp.arange(inner_len, dtype=jnp.int32)[None, :]
    phases = (row_ids * col_ids % period).astype(jnp.float32) * (2.0 * math.pi / period)
    return (cos_a, sin_a, cos_b, sin_b, jnp.cos(phases), jnp.sin(phases))


def forward_spectrum(signal, tables):
    cos_a, sin_a, cos_b, sin_b, tw_cos, tw_sin = tables
    outer_len = cos_a.shape[0]
    inner_len = cos_b.shape[0]
    half_len = outer_len // 2
    channels = signal.shape[0]
    grid_rows = signal.reshape(channels, half_len, inner_len)
    real_a = contract("cnb,kn->ckb", grid_rows, cos_a[:, :half_len])
    imag_a = -contract("cnb,kn->ckb", grid_rows, sin_a[:, :half_len])
    real_t = real_a * tw_cos + imag_a * tw_sin
    imag_t = imag_a * tw_cos - real_a * tw_sin
    real_s = contract("ckb,bm->ckm", real_t, cos_b) + contract("ckb,bm->ckm", imag_t, sin_b)
    imag_s = contract("ckb,bm->ckm", imag_t, cos_b) - contract("ckb,bm->ckm", real_t, sin_b)
    return (real_s, imag_s)


def inverse_signal(real_s, imag_s, tables):
    cos_a, sin_a, cos_b, sin_b, tw_cos, tw_sin = tables
    outer_len = cos_a.shape[0]
    inner_len = cos_b.shape[0]
    half_len = outer_len // 2
    channels = real_s.shape[0]
    real_z = contract("ckb,bm->ckm", real_s, cos_b) - contract("ckb,bm->ckm", imag_s, sin_b)
    imag_z = contract("ckb,bm->ckm", imag_s, cos_b) + contract("ckb,bm->ckm", real_s, sin_b)
    real_t = real_z * tw_cos - imag_z * tw_sin
    imag_t = imag_z * tw_cos + real_z * tw_sin
    signal = contract("ckb,kn->cnb", real_t, cos_a[:, :half_len]) - contract(
        "ckb,kn->cnb", imag_t, sin_a[:, :half_len]
    )
    scale_back = 1.0 / (outer_len * inner_len)
    return (signal * scale_back).reshape(channels, half_len * inner_len)


def channel_sum(values):
    return lax.psum(values, "ch")


def on_device(projections, grouped_short_filters, long_filter, norm_gain, out_grad):
    tokens = projections.shape[1]
    spread = lax.axis_size("ctx")
    length = tokens * spread
    outer_len, inner_len = factor_sizes(2 * length)
    tables = make_tables(outer_len, inner_len)
    per_chan = jnp.repeat(grouped_short_filters, GROUP, axis=2)
    edge_rows = passed_along(projections[:, tokens - (KS - 1) :, :], "ctx", 1)
    extended = jnp.concatenate([edge_rows, projections], axis=1)
    conv_sum = jnp.zeros(projections.shape, jnp.float32)
    for tap_idx in range(KS):
        window = extended[:, KS - 1 - tap_idx : KS - 1 - tap_idx + tokens, :].astype(jnp.float32)
        conv_sum = conv_sum + per_chan[:, tap_idx, None, :] * window
    features = lax.optimization_barrier(conv_sum.astype(jnp.bfloat16))
    gate_feat = features[0].astype(jnp.float32)
    key_feat = features[1].astype(jnp.float32)
    value_feat = features[2].astype(jnp.float32)
    mixed_in = key_feat * value_feat
    chan_h = lax.all_to_all(long_filter.T, "ctx", split_axis=0, concat_axis=1, tiled=True)
    chan_u = lax.all_to_all(mixed_in.T, "ctx", split_axis=0, concat_axis=1, tiled=True)
    real_u, imag_u = forward_spectrum(chan_u, tables)
    real_h, imaginary_filter = forward_spectrum(chan_h, tables)
    prod_r = real_u * real_h - imag_u * imaginary_filter
    prod_i = real_u * imaginary_filter + imag_u * real_h
    chan_z = inverse_signal(prod_r, prod_i, tables)
    conv_out = lax.all_to_all(chan_z, "ctx", split_axis=1, concat_axis=0, tiled=True).T
    gated_out = gate_feat * conv_out
    sq_total = channel_sum(jnp.sum(gated_out * gated_out, axis=1))
    rscale = lax.rsqrt(sq_total / D + epsilon)
    normed = gated_out * rscale[:, None]
    output = (normed * norm_gain).astype(jnp.bfloat16)
    gradient_float = out_grad.astype(jnp.float32)
    scaled = gradient_float * norm_gain
    inner_total = channel_sum(jnp.sum(scaled * normed, axis=1))
    grad_gated = rscale[:, None] * (scaled - normed * (inner_total / D)[:, None])
    gain_part = jnp.sum(gradient_float * normed, axis=0)
    grad_conv = grad_gated * gate_feat
    grad_gate = grad_gated * conv_out
    cotangent_gate_input = lax.all_to_all(
        grad_conv.T, "ctx", split_axis=0, concat_axis=1, tiled=True
    )
    real_d, imag_d = forward_spectrum(cotangent_gate_input, tables)
    back_r = real_h * real_d + imaginary_filter * imag_d
    back_i = real_h * imag_d - imaginary_filter * real_d
    filt_r = real_u * real_d + imag_u * imag_d
    filt_i = real_u * imag_d - imag_u * real_d
    chan_du = inverse_signal(back_r, back_i, tables)
    chan_dh = inverse_signal(filt_r, filt_i, tables)
    mix_back = lax.all_to_all(chan_du, "ctx", split_axis=1, concat_axis=0, tiled=True)
    filt_back = lax.all_to_all(chan_dh, "ctx", split_axis=1, concat_axis=0, tiled=True)
    grad_mix = mix_back.T
    long_grad = filt_back.T
    grad_feats = jnp.stack([grad_gate, grad_mix * value_feat, grad_mix * key_feat])
    next_rows = passed_along(grad_feats[:, : KS - 1, :], "ctx", -1)
    cotangent_widened = jnp.concatenate([grad_feats, next_rows], axis=1)
    grad_in = jnp.zeros(grad_feats.shape, jnp.float32)
    tap_terms = []
    local_width = projections.shape[2]
    for tap_idx in range(KS):
        grad_in = (
            grad_in
            + per_chan[:, tap_idx, None, :] * cotangent_widened[:, tap_idx : tap_idx + tokens, :]
        )
        window = extended[:, KS - 1 - tap_idx : KS - 1 - tap_idx + tokens, :].astype(jnp.float32)
        tap_prod = jnp.sum(grad_feats * window, axis=1)
        tap_terms.append(jnp.sum(tap_prod.reshape(3, local_width // GROUP, GROUP), axis=2))
    filt_part = jnp.stack(tap_terms, axis=1)
    gain_grad, short_grads = lax.psum((gain_part, filt_part), "ctx")
    return (output, grad_in.astype(jnp.bfloat16), short_grads, long_grad, gain_grad)


def solution(mesh):
    in_specs = (P(None, "ctx", "ch"), P(None, None, "ch"), P("ctx", "ch"), P("ch"), P("ctx", "ch"))
    out_specs = (P("ctx", "ch"), P(None, "ctx", "ch"), P(None, None, "ch"), P("ctx", "ch"), P("ch"))
    return jax.shard_map(
        on_device, mesh=mesh, in_specs=in_specs, out_specs=out_specs, check_vma=False
    )
```

profile of v0, /device:TPU:1, one launch (start us, length us, event | category | flops | bytes accessed | tf_op | source)
XLA Modules:
  0.0 527.5 jit_solution(2117349936834384752)
XLA Ops:
  1.5 4.6 collective-permute-start
  6.1 2.0 copy.90
  8.1 12.4 %all-to-all-start.1 = ((f32[64,16,128]{2,1,0:T(8,128)}), f32[64,16,128]{2,1,0:T(8,128)S(1)}, u32[]{:S(2)}, u32[]{:S(2)}) async-start(f32[64,16,128]{2,1,0:T(8,128)} %bitcast.13), calls=%async_computation.1 | async-start | bytes 1048576 | tf_op jit(solution)/shard_map/all_to_all | solution.py:106
  23.5 5.7 %fusion.6 = bf16[3,128,1024]{1,2,0:T(8,128)(2,1)S(1)} fusion(bf16[3,128,1024]{1,2,0:T(8,128)(2,1)S(1)} %copy.82, f32[3,1024]{1,0:T(4,128)S(1)} %get-tuple-element.51, f32[3,1024]{1,0:T(4,128)S(1)} %get-tuple-element.52, f32[3,1024]{1,0:T(4,128)S(1)} %get-tuple-element.53, f32[3,1024]{1,0:T(4,128)S(1)} %get-tuple-element.54, ...), kind=kLoop, calls=%fused_computation.31 | loop fusion | flops 15335424 | bytes 1695744 | tf_op jit(solution)/shard_map/convert_element_type | solution.py:101
  30.1 8.0 %all-to-all-done.1 = f32[64,16,128]{2,1,0:T(8,128)S(1)} async-done(((f32[64,16,128]{2,1,0:T(8,128)}), f32[64,16,128]{2,1,0:T(8,128)S(1)}, u32[]{:S(2)}, u32[]{:S(2)}) %all-to-all-start.1) | async-done | bytes 524320 | tf_op jit(solution)/shard_map/all_to_all | solution.py:106
  38.2 6.1 %all-to-all-start = ((f32[64,16,128]{2,1,0:T(8,128)}), f32[64,16,128]{2,1,0:T(8,128)}, u32[]{:S(2)}, u32[]{:S(2)}) async-start(f32[64,16,128]{2,1,0:T(8,128)} %bitcast.5), calls=%async_computation | async-start | bytes 1048576 | tf_op jit(solution)/shard_map/all_to_all | solution.py:107
  51.4 10.2 %all-to-all-done = f32[64,16,128]{2,1,0:T(8,128)} async-done(((f32[64,16,128]{2,1,0:T(8,128)}), f32[64,16,128]{2,1,0:T(8,128)}, u32[]{:S(2)}, u32[]{:S(2)}) %all-to-all-start) | async-done | bytes 524320 | tf_op jit(solution)/shard_map/all_to_all | solution.py:107
  61.6 2.1 convolution_negate_fusion.2
  63.7 2.1 fusion.85
  68.4 1.7 convolution_add_fusion.5
  70.1 2.5 multiply_subtract_fusion.3
  80.3 5.7 %all-to-all-start.2 = ((f32[16,64,128]{2,0,1:T(8,128)}), f32[16,64,128]{2,0,1:T(8,128)S(1)}, u32[]{:S(2)}, u32[]{:S(2)}) async-start(f32[16,64,128]{2,0,1:T(8,128)} %copy.104), calls=%async_computation.2 | async-start | bytes 1048576 | tf_op jit(solution)/shard_map/all_to_all | solution.py:113
  86.2 17.4 %all-to-all-done.2 = f32[16,64,128]{2,0,1:T(8,128)S(1)} async-done(((f32[16,64,128]{2,0,1:T(8,128)}), f32[16,64,128]{2,0,1:T(8,128)S(1)}, u32[]{:S(2)}, u32[]{:S(2)}) %all-to-all-start.2) | async-done | bytes 524320 | tf_op jit(solution)/shard_map/all_to_all | solution.py:113
  103.8 28.5 %psum.28 = f32[128]{0:T(128)S(1)} all-reduce(f32[128]{0:T(128)S(1)} %multiply_reduce_fusion), channel_id=1, replica_groups=mesh['ctx'=64,'ch'=8] {'ch'}, use_global_device_ids=true, to_apply=%region_1.2 | all-reduce | flops 128 | bytes 1024 | tf_op jit(solution)/shard_map/psum | solution.py:85
  133.3 20.3 %psum.29 = f32[128]{0:T(128)S(1)} all-reduce(f32[128]{0:T(128)S(1)} %get-tuple-element.23), channel_id=1, replica_groups=mesh['ctx'=64,'ch'=8] {'ch'}, use_global_device_ids=true, to_apply=%region_3.4 | all-reduce | flops 128 | bytes 1024 | tf_op jit(solution)/shard_map/psum | solution.py:85
  154.7 13.3 %all-to-all-start.3 = ((f32[64,16,128]{2,1,0:T(8,128)}), f32[64,16,128]{2,1,0:T(8,128)S(1)}, u32[]{:S(2)}, u32[]{:S(2)}) async-start(f32[64,16,128]{2,1,0:T(8,128)} %bitcast.36), calls=%async_computation.3 | async-start | bytes 1048576 | tf_op jit(solution)/shard_map/all_to_all | solution.py:126
  168.8 16.6 %all-to-all-done.3 = f32[64,16,128]{2,1,0:T(8,128)S(1)} async-done(((f32[64,16,128]{2,1,0:T(8,128)}), f32[64,16,128]{2,1,0:T(8,128)S(1)}, u32[]{:S(2)}, u32[]{:S(2)}) %all-to-all-start.3) | async-done | bytes 524320 | tf_op jit(solution)/shard_map/all_to_all | solution.py:126
  192.3 1.7 multiply_add_fusion
  194.1 2.2 fusion.123
  204.2 5.9 %all-to-all-start.4 = ((f32[16,64,128]{2,0,1:T(8,128)}), f32[16,64,128]{2,0,1:T(8,128)}, u32[]{:S(2)}, u32[]{:S(2)}) async-start(f32[16,64,128]{2,0,1:T(8,128)} %copy.115), calls=%async_computation.4 | async-start | bytes 1048576 | tf_op jit(solution)/shard_map/all_to_all | solution.py:136
  210.1 2.5 convolution_subtract_fusion
  217.8 9.8 %all-to-all-done.4 = f32[16,64,128]{2,0,1:T(8,128)} async-done(((f32[16,64,128]{2,0,1:T(8,128)}), f32[16,64,128]{2,0,1:T(8,128)}, u32[]{:S(2)}, u32[]{:S(2)}) %all-to-all-start.4) | async-done | bytes 524320 | tf_op jit(solution)/shard_map/all_to_all | solution.py:136
  227.6 6.3 %all-to-all-start.5 = ((f32[16,64,128]{2,0,1:T(8,128)}), f32[16,64,128]{2,0,1:T(8,128)}, u32[]{:S(2)}, u32[]{:S(2)}) async-start(f32[16,64,128]{2,0,1:T(8,128)} %copy.122), calls=%async_computation.5 | async-start | bytes 1048576 | tf_op jit(solution)/shard_map/all_to_all | solution.py:137
  235.1 7.3 %fusion.12 = (f32[3,1024]{1,0:T(4,128)S(1)}, f32[3,1024]{1,0:T(4,128)S(1)}, f32[3,1024]{1,0:T(4,128)S(1)}, f32[3,1024]{1,0:T(4,128)S(1)}, f32[3,1024]{1,0:T(4,12...) fusion(bf16[3,128,1024]{1,2,0:T(8,128)(2,1)S(1)} %copy-done.7, bf16[3,6,1024]{1,2,0:T(8,128)(2,1)} %copy-done.8, ...), kind=kLoop, calls=%fused_computation.37 | loop fusion | flops 16100352 | bytes 2482176 | tf_op jit(solution)/shard_map/reduce_sum | solution.py:152
  245.1 1.9 copy.116
  247.0 2.3 collective-permute-start.1
  249.3 1.9 all-to-all-done.5
  251.3 2.0 copy.126
  253.3 262.8 %all-reduce = (f32[3,7,64]{2,0,1:T(4,128)S(1)}, f32[1024]{0:T(1024)}) all-reduce(f32[3,7,64]{2,0,1:T(4,128)S(1)} %constant_dynamic-update-slice_fusion, f32[1024]{0:T(1024)S(1)} %copy-done.35), channel_id=1, replica_groups=mesh['ctx'=64,'ch'=8] {'ctx'}, use_global_device_ids=true, to_apply=%region_18.19 | all-reduce | flops 2368 | bytes 18944 | tf_op jit(solution)/shard_map/psum | solution.py:155
  516.7 1.7 copy.117
  518.4 1.7 pad_maximum_fusion
  520.2 5.9 %fusion.15 = bf16[3,128,1024]{1,2,0:T(8,128)(2,1)S(1)} fusion(f32[3,134,1024]{1,2,0:T(8,128)S(1)} %pad_maximum_fusion, f32[3,1024]{1,0:T(4,128)S(1)} %get-tuple-element.51, f32[3,1024]{1,0:T(4,128)S(1)} %copy-done.23, f32[3,1024]{1,0:T(4,128)S(1)} %copy-done.25, f32[3,1024]{1,0:T(4,128)S(1)} %copy-done.27, f32[3,1024]{1,0:T(4,128)S(1)} %copy-done.29, ...), kind=kLoop, calls=%fused_computation.41 | loop fusion | flops 6291456 | bytes 11882496 | tf_op jit(solution)/shard_map/convert_element_type | solution.py:156
  (157 shorter events, 50.4 us)
Async XLA Ops:
  0.6 20.7 %copy-start.36 = (f32[3,7,64]{2,1,0:T(8,128)S(1)}, f32[3,7,64]{2,1,0:T(8,128)}, u32[]{:S(2)}) copy-start(f32[3,7,64]{2,1,0:T(8,128)} %param.6) | copy-start | bytes 16132
  1.5 21.6 %collective-permute-start = (bf16[3,6,1024]{2,1,0:T(8,128)(2,1)S(1)}, bf16[3,6,1024]{2,1,0:T(8,128)(2,1)S(1)}, u32[]{:S(2)}, u32[]{:S(2)}) collective-permute-start(bf16[3,6,1024]{2,1,0:T(8,128)(2,1)S(1)} %slice.123), channel_id=1, source_target_pairs={{0,8},{8,16},{16,24},{24,32},{32,40},{40,48},{48,56},{56,64},{64,7... | collective-permute-start | bytes 110600 | tf_op jit(solution)/shard_map/ppermute | solution.py:19
  8.1 14.3 %copy-start.20 = (bf16[3,128,1024]{2,1,0:T(8,128)(2,1)S(1)}, bf16[3,128,1024]{2,1,0:T(8,128)(2,1)}, u32[]{:S(2)}) copy-start(bf16[3,128,1024]{2,1,0:T(8,128)(2,1)} %param.5) | copy-start | bytes 2359300
  8.1 30.1 %all-to-all-start.1 = ((f32[64,16,128]{2,1,0:T(8,128)}), f32[64,16,128]{2,1,0:T(8,128)S(1)}, u32[]{:S(2)}, u32[]{:S(2)}) async-start(f32[64,16,128]{2,1,0:T(8,128)} %bitcast.13), calls=%async_computation.1 | async-start | bytes 1048576 | tf_op jit(solution)/shard_map/all_to_all | solution.py:106
  20.8 24.5 %copy-start.15 = (f32[128,128]{0,1:T(8,128)}, f32[128,128]{0,1:T(8,128)S(1)}, u32[]{:S(2)}) copy-start(f32[128,128]{0,1:T(8,128)S(1)} %fusion.149) | copy-start | bytes 196612
  21.1 23.2 %copy-start.10 = (f32[128,128]{0,1:T(8,128)}, f32[128,128]{0,1:T(8,128)S(1)}, u32[]{:S(2)}) copy-start(f32[128,128]{0,1:T(8,128)S(1)} %fusion.148) | copy-start | bytes 196612
  22.1 7.1 %copy-start.22 = (f32[3,1024]{1,0:T(4,128)}, f32[3,1024]{1,0:T(4,128)S(1)}, u32[]{:S(2)}) copy-start(f32[3,1024]{1,0:T(4,128)S(1)} %get-tuple-element.52) | copy-start | bytes 36868
  22.1 7.1 %copy-start.24 = (f32[3,1024]{1,0:T(4,128)}, f32[3,1024]{1,0:T(4,128)S(1)}, u32[]{:S(2)}) copy-start(f32[3,1024]{1,0:T(4,128)S(1)} %get-tuple-element.53) | copy-start | bytes 36868
  22.1 7.1 %copy-start.26 = (f32[3,1024]{1,0:T(4,128)}, f32[3,1024]{1,0:T(4,128)S(1)}, u32[]{:S(2)}) copy-start(f32[3,1024]{1,0:T(4,128)S(1)} %get-tuple-element.54) | copy-start | bytes 36868
  22.1 7.1 %copy-start.28 = (f32[3,1024]{1,0:T(4,128)}, f32[3,1024]{1,0:T(4,128)S(1)}, u32[]{:S(2)}) copy-start(f32[3,1024]{1,0:T(4,128)S(1)} %get-tuple-element.55) | copy-start | bytes 36868
  22.1 7.1 %copy-start.30 = (f32[3,1024]{1,0:T(4,128)}, f32[3,1024]{1,0:T(4,128)S(1)}, u32[]{:S(2)}) copy-start(f32[3,1024]{1,0:T(4,128)S(1)} %get-tuple-element.56) | copy-start | bytes 36868
  22.8 6.5 %copy-start.6 = (bf16[3,128,1024]{1,2,0:T(8,128)(2,1)}, bf16[3,128,1024]{1,2,0:T(8,128)(2,1)S(1)}, u32[]{:S(2)}) copy-start(bf16[3,128,1024]{1,2,0:T(8,128)(2,1)S(1)} %copy.82) | copy-start | bytes 2359300
  23.0 6.2 %copy-start.32 = (f32[3,1,1024]{2,0,1:T(4,128)}, f32[3,1,1024]{2,0,1:T(4,128)S(1)}, u32[]{:S(2)}) copy-start(f32[3,1,1024]{2,0,1:T(4,128)S(1)} %copy.213) | copy-start | bytes 36868
  23.5 6.7 %copy-start.8 = (bf16[3,6,1024]{1,2,0:T(8,128)(2,1)}, bf16[3,6,1024]{1,2,0:T(8,128)(2,1)S(1)}, u32[]{:S(2)}) copy-start(bf16[3,6,1024]{1,2,0:T(8,128)(2,1)S(1)} %copy.83) | copy-start | bytes 110596
  38.2 23.4 %all-to-all-start = ((f32[64,16,128]{2,1,0:T(8,128)}), f32[64,16,128]{2,1,0:T(8,128)}, u32[]{:S(2)}, u32[]{:S(2)}) async-start(f32[64,16,128]{2,1,0:T(8,128)} %bitcast.5), calls=%async_computation | async-start | bytes 1048576 | tf_op jit(solution)/shard_map/all_to_all | solution.py:107
  50.2 19.9 %copy-start = (f32[16,128,128]{2,1,0:T(8,128)}, f32[16,128,128]{2,1,0:T(8,128)S(1)}, u32[]{:S(2)}) copy-start(f32[16,128,128]{2,1,0:T(8,128)S(1)} %convolution_subtract_fusion.4) | copy-start | bytes 3145732
  50.2 11.4 %copy-start.11 = (f32[128,128]{0,1:T(8,128)S(1)}, f32[128,128]{0,1:T(8,128)}, u32[]{:S(2)}) copy-start(f32[128,128]{0,1:T(8,128)} %copy-done.10) | copy-start | bytes 196612
  51.4 18.7 %copy-start.2 = (f32[16,128,128]{2,1,0:T(8,128)}, f32[16,128,128]{2,1,0:T(8,128)S(1)}, u32[]{:S(2)}) copy-start(f32[16,128,128]{2,1,0:T(8,128)S(1)} %convolution_add_fusion.4) | copy-start | bytes 3145732
  51.4 12.3 %copy-start.16 = (f32[128,128]{0,1:T(8,128)S(1)}, f32[128,128]{0,1:T(8,128)}, u32[]{:S(2)}) copy-start(f32[128,128]{0,1:T(8,128)} %copy-done.15) | copy-start | bytes 196612
  70.1 2.5 copy-start.4
  79.2 6.8 %copy-start.21 = (bf16[128,1024]{1,0:T(8,128)(2,1)S(1)}, bf16[128,1024]{1,0:T(8,128)(2,1)}, u32[]{:S(2)}) copy-start(bf16[128,1024]{1,0:T(8,128)(2,1)} %param.9) | copy-start | bytes 786436
  79.2 53.1 %copy-start.34 = (f32[1024]{0:T(1024)S(1)}, f32[1024]{0:T(1024)}, u32[]{:S(2)}) copy-start(f32[1024]{0:T(1024)} %param.8) | copy-start | bytes 12292
  80.3 23.3 %all-to-all-start.2 = ((f32[16,64,128]{2,0,1:T(8,128)}), f32[16,64,128]{2,0,1:T(8,128)S(1)}, u32[]{:S(2)}, u32[]{:S(2)}) async-start(f32[16,64,128]{2,0,1:T(8,128)} %copy.104), calls=%async_computation.2 | async-start | bytes 1048576 | tf_op jit(solution)/shard_map/all_to_all | solution.py:113
  154.7 31.9 %copy-start.17 = (f32[128,128]{0,1:T(8,128)S(1)}, f32[128,128]{0,1:T(8,128)}, u32[]{:S(2)}) copy-start(f32[128,128]{0,1:T(8,128)} %copy-done.15) | copy-start | bytes 196612
  154.7 30.8 %all-to-all-start.3 = ((f32[64,16,128]{2,1,0:T(8,128)}), f32[64,16,128]{2,1,0:T(8,128)S(1)}, u32[]{:S(2)}, u32[]{:S(2)}) async-start(f32[64,16,128]{2,1,0:T(8,128)} %bitcast.36), calls=%async_computation.3 | async-start | bytes 1048576 | tf_op jit(solution)/shard_map/all_to_all | solution.py:126
  190.1 1.8 copy-start.5
  190.1 2.1 copy-start.9
  204.2 23.4 %all-to-all-start.4 = ((f32[16,64,128]{2,0,1:T(8,128)}), f32[16,64,128]{2,0,1:T(8,128)}, u32[]{:S(2)}, u32[]{:S(2)}) async-start(f32[16,64,128]{2,0,1:T(8,128)} %copy.115), calls=%async_computation.4 | async-start | bytes 1048576 | tf_op jit(solution)/shard_map/all_to_all | solution.py:136
  217.8 17.3 %copy-start.7 = (bf16[3,128,1024]{1,2,0:T(8,128)(2,1)S(1)}, bf16[3,128,1024]{1,2,0:T(8,128)(2,1)}, u32[]{:S(2)}) copy-start(bf16[3,128,1024]{1,2,0:T(8,128)(2,1)} %copy-done.6) | copy-start | bytes 2359300
  227.6 23.7 %all-to-all-start.5 = ((f32[16,64,128]{2,0,1:T(8,128)}), f32[16,64,128]{2,0,1:T(8,128)}, u32[]{:S(2)}, u32[]{:S(2)}) async-start(f32[16,64,128]{2,0,1:T(8,128)} %copy.122), calls=%async_computation.5 | async-start | bytes 1048576 | tf_op jit(solution)/shard_map/all_to_all | solution.py:137
  244.7 8.6 %copy-start.35 = (f32[1024]{0:T(1024)S(1)}, f32[1024]{0:T(1024)}, u32[]{:S(2)}) copy-start(f32[1024]{0:T(1024)} %get-tuple-element.22) | copy-start | bytes 12292
  247.0 269.7 %collective-permute-start.1 = (f32[3,6,1024]{2,1,0:T(8,128)S(1)}, f32[3,6,1024]{2,1,0:T(8,128)S(1)}, u32[]{:S(2)}, u32[]{:S(2)}) collective-permute-start(f32[3,6,1024]{2,1,0:T(8,128)S(1)} %copy.116), channel_id=1, source_target_pairs={{8,0},{16,8},{24,16},{32,24},{40,32},{48,40},{56,48},{64,56},{72,6... | collective-permute-start | bytes 221192 | tf_op jit(solution)/shard_map/ppermute | solution.py:19
  (13 other events, 18.4 us)
where the time goes:
time: 538 us; the launch traced here: 527 us
  blocking collectives  312 us (58%)
  waiting for transfers between devices  64 us (12%)
  starting transfers between devices  56.6 us (11%)
  matrix products  47.7 us (9%)
  other arithmetic  27.8 us (5%)
  local copies, waits for them, and re-layouts  17.9 us (3%)
    psum x1, blocking collectives, on_device(): gain_grad, short_grads = lax.psum((gain_part, filt_part), 'ctx')  263 us
    psum x2, blocking collectives, channel_sum(): return lax.psum(values, 'ch')  48.8 us
    dot_general x36, matrix products, contract(): return jnp.einsum(form, left, right, precision=lax.Precision.HIGHEST)  47.7 us
    all_to_all x1, waiting for transfers between devices, on_device(): lax.all_to_all(chan_z, 'ctx', split_axis=1, concat_axis=0, tiled=True)  17.4 us
    all_to_all x1, waiting for transfers between devices, on_device(): lax.all_to_all(grad_conv.T, 'ctx', split_axis=0, concat_axis=1, tiled=True)  16.6 us
    all_to_all x1, starting transfers between devices, on_device(): lax.all_to_all(grad_conv.T, 'ctx', split_axis=0, concat_axis=1, tiled=True)  13.3 us
    all_to_all x1, starting transfers between devices, on_device(): lax.all_to_all(long_filter.T, 'ctx', split_axis=0, concat_axis=1, tiled=T...  12.4 us
  transfers between devices with their start and end apart: 8, of which 6 were waited for; matrix products, arithmetic and copies ran while one was open for 8% of the time, Pallas kernels for 0%

commit v1 on v0

v1 whole, which is shorter than its diff:
```python
import functools
import math

import jax
import jax.numpy as jnp
import numpy as np
from jax import lax
from jax.experimental import pallas as pl
from jax.experimental.pallas import tpu as pltpu
from jax.sharding import PartitionSpec as P

D = 8192
GROUP = 16
KS = 7
EPS = 1e-05
MESH = pl.DeviceIdType.MESH
F32 = jnp.float32
BF16 = jnp.bfloat16

NT = 128
NC = 1024
NP = 64
NH = 8
CH = NC // NP
NB = NC // 128
NG = NC // GROUP

X_H, X_U, X_Z, X_D, X_DU, X_DH = range(6)


def split_np(a):
    hi = a.astype(jnp.bfloat16)
    lo = (a - hi.astype(np.float64)).astype(jnp.bfloat16)
    return hi, lo


@functools.lru_cache(maxsize=None)
def tables():
    n1 = np.arange(NP)[None, :]
    k1 = np.arange(NP)[:, None]
    ang = 2 * math.pi * ((n1 * (4 * k1 + 1)) % (4 * NP)) / (4 * NP)
    wa = np.concatenate([np.cos(ang), -np.sin(ang)], axis=0)
    wah, wal = split_np(wa)
    iah, ial = split_np(wa.T / (NP * NT))
    n2 = np.arange(NT)[None, :]
    tw = 2 * math.pi * (n2 * (4 * k1 + 1)) / (4 * NP * NT)
    tr = np.cos(tw).astype(np.float32)
    ti = (-np.sin(tw)).astype(np.float32)
    m = np.arange(NT)
    angb = 2 * math.pi * ((m[:, None] * m[None, :]) % NT) / NT
    c, s = np.cos(angb), np.sin(angb)
    mb = np.block([[c, -s], [s, c]])
    mbh, mbl = split_np(mb)
    ibh, ibl = split_np(mb.T)
    return (
        np.concatenate([wah, wal], axis=1),
        np.concatenate([iah, iah, ial], axis=1),
        mbh, mbl, ibh, ibl, tr, ti,
    )


def split(x):
    hi = x.astype(BF16)
    return hi, (x - hi.astype(F32)).astype(BF16)


def dot(a, b):
    return jnp.dot(a, b, preferred_element_type=F32)


def lanes(b):
    return pl.ds(pl.multiple_of(b * 128, 128), 128)


def kernel(
    proj_hbm, gsf, h_hbm, gain, og_hbm, wa_in, ia_in, mbh_in, mbl_in, ibh_in, ibl_in, tr_in, ti_in,
    out, pg, sg, lg, gg,
    pv, hv, ogv, wa, ia, mbh, mbl, ibh, ibl, tr, ti,
    halo, ext, gext, kf, vf, qT, scT, G, pc, taps, sb, rb, F, bh, bl, SH, SU, SD, SP,
    nsb, nrb, ar1, ar1r, ar1s, ar1q, ar2, ar2r, ar2s, ar2q,
    in_sem, xs, xr, hs, hr, ns, nr, as_, ar_,
):
    me = lax.axis_index("ctx")
    mc = lax.axis_index("ch")
    bar = pltpu.get_barrier_semaphore()

    loads = [
        pltpu.make_async_copy(a, b, in_sem.at[k])
        for k, (a, b) in enumerate([
            (h_hbm, hv), (proj_hbm, pv), (og_hbm, ogv), (wa_in, wa), (ia_in, ia), (mbh_in, mbh),
            (mbl_in, mbl), (ibh_in, ibh), (ibl_in, ibl), (tr_in, tr), (ti_in, ti)])
    ]
    for c in loads:
        c.start()

    def greet(i, _):
        pl.semaphore_signal(bar, inc=1, device_id={"ctx": lax.rem(me + i, NP)}, device_id_type=MESH)
        return _

    lax.fori_loop(1, NP, greet, 0)

    def greet_ch(i, _):
        pl.semaphore_signal(bar, inc=1, device_id={"ch": lax.rem(mc + i, NH)}, device_id_type=MESH)
        return _

    lax.fori_loop(1, NH, greet_ch, 0)

    def rows16(i):
        return pl.ds(pl.multiple_of(i * CH, CH), CH)

    def send_to(k, t):
        return pltpu.make_async_remote_copy(
            src_ref=sb.at[k, rows16(t)], dst_ref=rb.at[k, rows16(me)],
            send_sem=xs.at[k], recv_sem=xr.at[k], device_id={"ctx": t}, device_id_type=MESH)

    def exchange(k):
        def one(i, _):
            send_to(k, lax.rem(me + i, NP)).start()
            return _

        lax.fori_loop(1, NP, one, 0)
        pltpu.make_async_copy(sb.at[k, rows16(me)], rb.at[k, rows16(me)], xr.at[k]).start()

    def arrived(k):
        pltpu.make_async_copy(rb.at[k], rb.at[k], xr.at[k]).wait()

    def sent(k):
        part = sb.at[k, pl.ds(0, NC - CH)]
        pltpu.make_async_copy(part, part, xs.at[k]).wait()

    loads[0].wait()

    def h_block(b, _):
        sb[X_H, pl.ds(pl.multiple_of(b * 128, 128), 128), :] = hv[:, lanes(b)].T.astype(BF16)
        return _

    lax.fori_loop(0, NB, h_block, 0)
    loads[1].wait()

    pl.semaphore_wait(bar, NP - 1 + NH - 1)

    nxt = lax.rem(me + 1, NP)
    prv = lax.rem(me + NP - 1, NP)
    halo_copy = pltpu.make_async_remote_copy(
        src_ref=pv.at[:, pl.ds(NT - 16, 16), :], dst_ref=halo, send_sem=hs.at[0], recv_sem=hr.at[0],
        device_id={"ctx": nxt}, device_id_type=MESH)
    halo_copy.start()
    exchange(X_H)

    member = (
        lax.broadcasted_iota(jnp.int32, (NG, NC), 1) // GROUP
        == lax.broadcasted_iota(jnp.int32, (NG, NC), 0)
    ).astype(F32)
    for i in range(3):
        pc[i, pl.ds(0, KS), :] = jnp.dot(
            gsf[i], member, preferred_element_type=F32, precision=lax.Precision.HIGHEST)
        ext[i, pl.ds(8, NT), :] = pv[i].astype(F32)
    loads[2].wait()

    halo_copy.wait()
    first = jnp.where(me == 0, 0.0, 1.0).astype(F32)
    for i in range(3):
        edge = halo[i].astype(F32)
        ext[i, pl.ds(0, 8), :] = jnp.where(me == 0, 0.0, edge[8:, :])

    def feat_block(b, _):
        L = lanes(b)
        f = []
        for i in range(3):
            acc = pc[i, pl.ds(0, 1), L] * ext[i, pl.ds(8, NT), L]
            for j in range(1, KS):
                acc = acc + pc[i, pl.ds(j, 1), L] * ext[i, pl.ds(8 - j, NT), L]
            f.append(acc.astype(BF16).astype(F32))
        R = pl.ds(pl.multiple_of(b * 128, 128), 128)
        sb[X_U, R, :] = (f[1] * f[2]).T.astype(BF16)
        kf[:, L] = f[1]
        vf[:, L] = f[2]
        qT[R, :] = f[0].T
        return _

    lax.fori_loop(0, NB, feat_block, 0)
    exchange(X_U)

    def sc_block(b, _):
        L = lanes(b)
        R = pl.ds(pl.multiple_of(b * 128, 128), 128)
        scT[R, :] = (ogv[:, L].astype(F32) * gain[pl.ds(b, 1), :]).T
        return _

    lax.fori_loop(0, NB, sc_block, 0)
    for c in loads[3:]:
        c.wait()

    def forward(k, S):
        F[...] = rb[k].astype(F32)

        def pair(g, _):
            x = jnp.concatenate(
                [F[pl.ds(2 * g + e, NP, stride=CH), :] for e in range(2)], axis=1).astype(BF16)
            a = dot(wa[...], jnp.concatenate([x, x], axis=0))
            for e in range(2):
                ar = a[:NP, e * NT:(e + 1) * NT]
                ai = a[NP:, e * NT:(e + 1) * NT]
                br = ar * tr[...] - ai * ti[...]
                bi = ar * ti[...] + ai * tr[...]
                hi, lo = split(jnp.concatenate([br, bi], axis=1))
                R = pl.ds(pl.multiple_of((2 * g + e) * NP, NP), NP)
                bh[R, :] = hi
                bl[R, :] = lo
            return _

        lax.fori_loop(0, CH // 2, pair, 0)

        def block(r, _):
            R = pl.ds(pl.multiple_of(r * 256, 256), 256)
            S[R, :] = (
                dot(bh[R, :], mbh[...]) + dot(bh[R, :], mbl[...]) + dot(bl[R, :], mbh[...]))
            return _

        lax.fori_loop(0, NC // 256, block, 0)

    def inverse(k, A, B, conj):
        def block(r, _):
            R = pl.ds(pl.multiple_of(r * 256, 256), 256)
            a_r, a_i = A[R, pl.ds(0, NT)], A[R, pl.ds(NT, NT)]
            b_r, b_i = B[R, pl.ds(0, NT)], B[R, pl.ds(NT, NT)]
            if conj:
                p_r = a_r * b_r + a_i * b_i
                p_i = a_r * b_i - a_i * b_r
            else:
                p_r = a_r * b_r - a_i * b_i
                p_i = a_r * b_i + a_i * b_r
            hi, lo = split(jnp.concatenate([p_r, p_i], axis=1))
            SP[R, :] = dot(hi, ibh[...]) + dot(hi, ibl[...]) + dot(lo, ibh[...])
            return _

        lax.fori_loop(0, NC // 256, block, 0)

        def pair(g, _):
            cols = []
            for e in range(2):
                R = pl.ds(pl.multiple_of((2 * g + e) * NP, NP), NP)
                cr, ci = SP[R, pl.ds(0, NT)], SP[R, pl.ds(NT, NT)]
                dr = cr * tr[...] + ci * ti[...]
                di = ci * tr[...] - cr * ti[...]
                cols.append(jnp.concatenate([dr, di], axis=0))
            hi, lo = split(jnp.concatenate(cols, axis=1))
            z = dot(ia[...], jnp.concatenate([hi, lo, hi], axis=0))
            for e in range(2):
                F[pl.ds(2 * g + e, NP, stride=CH), :] = z[:, e * NT:(e + 1) * NT]
            return _

        lax.fori_loop(0, CH // 2, pair, 0)
        sb[k] = F[...].astype(BF16)

    arrived(X_H)
    forward(X_H, SH)
    arrived(X_U)
    forward(X_U, SU)
    inverse(X_Z, SU, SH, False)
    exchange(X_Z)
    arrived(X_Z)

    def gate_block(b, carry):
        s1, s2 = carry
        R = pl.ds(pl.multiple_of(b * 128, 128), 128)
        g = qT[R, :] * rb[X_Z, R, :].astype(F32)
        G[R, :] = g
        return s1 + jnp.sum(g * g, axis=0, keepdims=True), s2 + jnp.sum(
            g * scT[R, :], axis=0, keepdims=True)

    zero = jnp.zeros((1, NT), F32)
    s1, s2 = lax.fori_loop(0, NB, gate_block, (zero, zero))
    row = lax.broadcasted_iota(jnp.int32, (8, NT), 0)
    nsb[...] = jnp.where(row == 0, s1, jnp.where(row == 1, s2, 0.0))

    def group_sum(src, dst, ssem, rsem, mine, size, target):
        def one(i, _):
            j = lax.rem(mine + i, size)
            pltpu.make_async_remote_copy(
                src_ref=src, dst_ref=dst.at[mine], send_sem=ssem, recv_sem=rsem,
                device_id=target(j), device_id_type=MESH).start()
            return _

        lax.fori_loop(1, size, one, 0)
        pltpu.make_async_copy(src, dst.at[mine], rsem).start()

    def group_wait(dst, rsem):
        pltpu.make_async_copy(dst, dst, rsem).wait()
        total = dst[0]
        for i in range(1, dst.shape[0]):
            total = total + dst[i]
        return total

    def group_sent(dst, ssem, size):
        part = dst.at[pl.ds(0, size - 1)]
        pltpu.make_async_copy(part, part, ssem).wait()

    group_sum(nsb, nrb, ns, nr, mc, NH, lambda j: {"ch": j})
    tot = group_wait(nrb, nr)
    rs = lax.rsqrt(tot[0:1] / D + EPS)
    inner = rs * tot[1:2] / D
    coef = rs * rs * inner

    def d_block(b, _):
        R = pl.ds(pl.multiple_of(b * 128, 128), 128)
        q = qT[R, :]
        g = G[R, :]
        grad = rs * scT[R, :] - coef * g
        sb[X_D, R, :] = (grad * q).astype(BF16)
        return _

    lax.fori_loop(0, NB, d_block, 0)
    exchange(X_D)

    def out_block(b, _):
        L = lanes(b)
        R = pl.ds(pl.multiple_of(b * 128, 128), 128)
        g = G[R, :]
        normed = (g * rs).T
        out[:, L] = (normed * gain[pl.ds(b, 1), :]).astype(BF16)
        ar1[pl.ds(b, 1), :] = jnp.sum(ogv[:, L].astype(F32) * normed, axis=0, keepdims=True)
        grad = rs * scT[R, :] - coef * g
        gext[0, pl.ds(0, NT), L] = (grad * rb[X_Z, R, :].astype(F32)).T
        return _

    lax.fori_loop(0, NB, out_block, 0)

    def edge_copy(lo, n, s):
        return pltpu.make_async_remote_copy(
            src_ref=gext.at[pl.ds(lo, n), pl.ds(0, 8), :],
            dst_ref=gext.at[pl.ds(lo, n), pl.ds(NT, 8), :],
            send_sem=hs.at[s], recv_sem=hr.at[s], device_id={"ctx": prv}, device_id_type=MESH)

    edge0 = edge_copy(0, 1, 1)
    edge0.start()

    def taps_of(i):
        def block(b, _):
            L = lanes(b)
            g = gext[i, pl.ds(0, NT), L]
            for j in range(KS):
                taps[i, pl.ds(j, 1), L] = jnp.sum(
                    g * ext[i, pl.ds(8 - j, NT), L], axis=0, keepdims=True)
            taps[i, pl.ds(KS, 1), L] = jnp.zeros((1, 128), F32)
            return _

        lax.fori_loop(0, NB, block, 0)
        return lax.dot_general(
            taps[i], member, (((1,), (1,)), ((), ())), preferred_element_type=F32,
            precision=lax.Precision.HIGHEST)

    def short_back(i):
        gext[i, pl.ds(NT, 8), :] = jnp.where(me == NP - 1, 0.0, gext[i, pl.ds(NT, 8), :])

        def block(b, _):
            L = lanes(b)
            acc = pc[i, pl.ds(0, 1), L] * gext[i, pl.ds(0, NT), L]
            for j in range(1, KS):
                acc = acc + pc[i, pl.ds(j, 1), L] * gext[i, pl.ds(j, NT), L]
            pg[i, :, L] = acc.astype(BF16)
            return _

        lax.fori_loop(0, NB, block, 0)

    my_y = lax.rem(me // 2, 8)
    my_zc = (me // 16) * 2 + lax.rem(me, 2)

    def y_peer(j):
        return {"ctx": (me // 16) * 16 + j * 2 + lax.rem(me, 2)}

    def zc_peer(j):
        return {"ctx": (j // 2) * 16 + my_y * 2 + lax.rem(j, 2)}

    t0 = taps_of(0)
    ar1[pl.ds(8, 8), :] = jnp.concatenate([t0, jnp.zeros((8, 128 - NG), F32)], axis=1)
    group_sum(ar1, ar1r, as_.at[0], ar_.at[0], my_y, 8, y_peer)

    arrived(X_D)
    forward(X_D, SD)
    inverse(X_DU, SH, SD, True)
    exchange(X_DU)
    inverse(X_DH, SU, SD, True)
    exchange(X_DH)

    ar1s[...] = group_wait(ar1r, ar_.at[0])
    group_sum(ar1s, ar1q, as_.at[1], ar_.at[1], my_zc, 8, zc_peer)
    edge0.wait()
    short_back(0)

    arrived(X_DU)

    def mix_block(b, _):
        L = lanes(b)
        R = pl.ds(pl.multiple_of(b * 128, 128), 128)
        m = rb[X_DU, R, :].astype(F32).T
        gext[1, pl.ds(0, NT), L] = m * vf[:, L]
        gext[2, pl.ds(0, NT), L] = m * kf[:, L]
        return _

    lax.fori_loop(0, NB, mix_block, 0)
    edge12 = edge_copy(1, 2, 2)
    edge12.start()
    t1 = taps_of(1)
    t2 = taps_of(2)
    ar2[...] = jnp.concatenate([t1, t2], axis=1)
    group_sum(ar2, ar2r, as_.at[2], ar_.at[2], my_y, 8, y_peer)
    edge12.wait()
    short_back(1)
    ar2s[...] = group_wait(ar2r, ar_.at[2])
    group_sum(ar2s, ar2q, as_.at[3], ar_.at[3], my_zc, 8, zc_peer)
    short_back(2)

    arrived(X_DH)

    def filt_block(b, _):
        R = pl.ds(pl.multiple_of(b * 128, 128), 128)
        lg[:, lanes(b)] = rb[X_DH, R, :].astype(F32).T
        return _

    lax.fori_loop(0, NB, filt_block, 0)

    a1 = group_wait(ar1q, ar_.at[1])
    gg[...] = a1[0:8]
    sg[0] = a1[8:8 + KS, 0:NG]
    a2 = group_wait(ar2q, ar_.at[3])
    sg[1] = a2[0:KS, 0:NG]
    sg[2] = a2[0:KS, NG:]

    for k in range(6):
        sent(k)
    group_sent(nrb, ns, NH)
    group_sent(ar1r, as_.at[0], 8)
    group_sent(ar1q, as_.at[1], 8)
    group_sent(ar2r, as_.at[2], 8)
    group_sent(ar2q, as_.at[3], 8)


def on_device(projections, grouped_short_filters, long_filter, norm_gain, out_grad):
    anywhere = pl.BlockSpec(memory_space=pl.ANY)
    vmem = pl.BlockSpec(memory_space=pltpu.VMEM)
    tabs = tables()
    dma = pltpu.SemaphoreType.DMA
    res = pl.pallas_call(
        kernel,
        out_shape=[
            jax.ShapeDtypeStruct((NT, NC), BF16),
            jax.ShapeDtypeStruct((3, NT, NC), BF16),
            jax.ShapeDtypeStruct((3, KS, NG), F32),
            jax.ShapeDtypeStruct((NT, NC), F32),
            jax.ShapeDtypeStruct((8, 128), F32),
        ],
        in_specs=[anywhere, vmem, anywhere, vmem, anywhere] + [anywhere] * 8,
        out_specs=[vmem] * 5,
        scratch_shapes=[
            pltpu.VMEM((3, NT, NC), BF16),
            pltpu.VMEM((NT, NC), F32),
            pltpu.VMEM((NT, NC), BF16),
            *[pltpu.VMEM(t.shape, t.dtype) for t in tabs],
            pltpu.VMEM((3, 16, NC), BF16),
            pltpu.VMEM((3, NT + 8, NC), F32),
            pltpu.VMEM((3, NT + 8, NC), F32),
            pltpu.VMEM((NT, NC), F32),
            pltpu.VMEM((NT, NC), F32),
            pltpu.VMEM((NC, NT), F32),
            pltpu.VMEM((NC, NT), F32),
            pltpu.VMEM((NC, NT), F32),
            pltpu.VMEM((3, 8, NC), F32),
            pltpu.VMEM((3, 8, NC), F32),
            pltpu.VMEM((6, NC, NT), BF16),
            pltpu.VMEM((6, NC, NT), BF16),
            pltpu.VMEM((NC, NT), F32),
            pltpu.VMEM((NC, 2 * NT), BF16),
            pltpu.VMEM((NC, 2 * NT), BF16),
            *[pltpu.VMEM((NC, 2 * NT), F32)] * 4,
            pltpu.VMEM((8, 128), F32),
            pltpu.VMEM((NH, 8, 128), F32),
            pltpu.VMEM((16, 128), F32),
            pltpu.VMEM((8, 16, 128), F32),
            pltpu.VMEM((16, 128), F32),
            pltpu.VMEM((8, 16, 128), F32),
            pltpu.VMEM((8, 128), F32),
            pltpu.VMEM((8, 8, 128), F32),
            pltpu.VMEM((8, 128), F32),
            pltpu.VMEM((8, 8, 128), F32),
            dma((11,)), dma((6,)), dma((6,)), dma((3,)), dma((3,)), dma, dma, dma((4,)), dma((4,)),
        ],
        compiler_params=pltpu.CompilerParams(
            collective_id=0, has_side_effects=True, vmem_limit_bytes=56 * 2**20),
    )(projections, grouped_short_filters, long_filter, norm_gain.reshape(8, 128), out_grad,
      *[jnp.asarray(t) for t in tabs])
    out, pg, sg, lg, gg = res
    return out, pg, sg, lg, gg.reshape(NC)


def solution(mesh):
    in_specs = (P(None, "ctx", "ch"), P(None, None, "ch"), P("ctx", "ch"), P("ch"), P("ctx", "ch"))
    out_specs = (P("ctx", "ch"), P(None, "ctx", "ch"), P(None, None, "ch"), P("ctx", "ch"), P("ch"))
    return jax.shard_map(
        on_device, mesh=mesh, in_specs=in_specs, out_specs=out_specs, check_vma=False
    )
```

time: 538 us -> 104 us (0.19); the launches traced: 527 us -> 104 us
  blocking collectives: 312 us -> 0 us
  Pallas kernels: 0 us -> 97.1 us
  waiting for transfers between devices: 64 us -> 0 us
  starting transfers between devices: 56.6 us -> 0 us
  matrix products: 47.7 us -> 0 us
  other arithmetic: 27.8 us -> 0 us
  local copies, waits for them, and re-layouts: 17.9 us -> 5.79 us
    psum x3 -> x0, blocking collectives: 312 us -> none  [the longest x1 263 us: on_device(): gain_grad, short_grads = lax.psum((gain_part, filt_part), 'ctx')]
    pallas_call x0 -> x1, Pallas kernels: none -> 97.1 us  [on_device(): pl.pallas_call(kernel, out_shape=[jax.ShapeDtypeStruct((NT, NC), BF16), j...]
    all_to_all x6 -> x0, waiting for transfers between devices: 64 us -> none  [the longest x1 17.4 us: on_device(): lax.all_to_all(chan_z, 'ctx', split_axis=1, concat_axis=0, tiled=True)]
    all_to_all x6 -> x0, starting transfers between devices: 49.7 us -> none  [the longest x1 13.3 us: on_device(): lax.all_to_all(grad_conv.T, 'ctx', split_axis=0, concat_axis=1, tiled=True)]
    dot_general x36 -> x0, matrix products: 47.7 us -> none  [contract(): return jnp.einsum(form, left, right, precision=lax.Precision.HIGHEST)]
    convert_element_type x2 -> x0, other arithmetic: 11.6 us -> none  [the longest x1 5.87 us: on_device(): grad_in.astype(jnp.bfloat16)]
    reduce_sum x10 -> x0, other arithmetic: 9.11 us -> none  [the longest x1 7.29 us: on_device(): tap_prod = jnp.sum(grad_feats * window, axis=1)]
    ppermute x2 -> x0, starting transfers between devices: 6.85 us -> none  [passed_along(): return lax.ppermute(block, axis, route)]
  transfers between devices with their start and end apart: 8 -> 0, of which waited for: 6 -> 0; matrix products, arithmetic and copies ran while one was open for 8% -> 0% of each run, Pallas kernels for 0% -> 0%
where the time goes in v1:
time: 104 us
  Pallas kernels  97.1 us (93%)
  local copies, waits for them, and re-layouts  5.79 us (6%)
    pallas_call x1, Pallas kernels, on_device(): pl.pallas_call(kernel, out_shape=[jax.ShapeDtypeStruct((NT, NC), BF16), j...  97.1 us
    unnamed x11, local copies, waits for them, and re-layouts  5.79 us

profile of v1, /device:TPU:1, one launch (start us, length us, event | category | flops | bytes accessed | tf_op | source)
XLA Modules:
  0.0 103.5 jit_solution(13761206309212957889)
XLA Ops:
  0.6 97.1 %shard_map.164 = (bf16[128,1024]{1,0:T(8,128)(2,1)}, bf16[3,128,1024]{2,1,0:T(8,128)(2,1)}, f32[3,7,64]{2,1,0:T(8,128)}, f32[128,1024]{1,0:T(8,128)}, f32[8,128]{1,0:T(8,128)}) custom-call(bf16[3,128,1024]{2,1,0:T(8,128)(2,1)} %proj_hbm.1, f32[3,7,64]{2,1,0:T(8,128)} %gsf.1, f32[128,1024]{1,0:T(8,128)} %h_hbm.1, f32[8,128]{1,0:T(8,128)} %bitcast.2, ...), custom_call_target="tpu_custom_call" | custom-call | tf_op jit(solution)/shard_map/pallas_call | solution.py:444
  97.7 1.7 %copy.23 = bf16[128,1024]{1,0:T(8,128)(2,1)} copy(bf16[128,1024]{1,0:T(8,128)(2,1)} %get-tuple-element.20) | data formatting | bytes 524288
  99.4 0.0 copy-start.1
  99.4 0.0 copy-start
  99.4 2.1 %copy.24 = bf16[3,128,1024]{2,1,0:T(8,128)(2,1)} copy(bf16[3,128,1024]{2,1,0:T(8,128)(2,1)} %get-tuple-element.21) | data formatting | bytes 1572864
  101.5 0.0 copy-done.1
  101.5 0.6 copy.25
  102.1 0.0 copy-done
  102.1 0.0 copy-start.2
  102.1 0.8 copy.26
  102.9 0.0 copy-done.2
  102.9 0.6 copy.27
Async XLA Ops:
  99.4 2.1 %copy-start.1 = (f32[3,7,64]{2,1,0:T(8,128)S(1)}, f32[3,7,64]{2,1,0:T(8,128)}, u32[]{:S(2)}) copy-start(f32[3,7,64]{2,1,0:T(8,128)} %get-tuple-element.22) | copy-start | bytes 16132
  99.4 2.7 %copy-start = (f32[128,1024]{1,0:T(8,128)S(1)}, f32[128,1024]{1,0:T(8,128)}, u32[]{:S(2)}) copy-start(f32[128,1024]{1,0:T(8,128)} %get-tuple-element.23) | copy-start | bytes 1572868
  102.1 0.8 copy-start.2

commit v2 on v1

--- a/solution.py
+++ b/solution.py
@@ -24,6 +24,8 @@
 CH = NC // NP
 NB = NC // 128
 NG = NC // GROUP
+UNP = 4
+UNB = 4
 
 X_H, X_U, X_Z, X_D, X_DU, X_DH = range(6)
 
@@ -74,8 +76,8 @@
 
 def kernel(
     proj_hbm, gsf, h_hbm, gain, og_hbm, wa_in, ia_in, mbh_in, mbl_in, ibh_in, ibl_in, tr_in, ti_in,
-    out, pg, sg, lg, gg,
-    pv, hv, ogv, wa, ia, mbh, mbl, ibh, ibl, tr, ti,
+    out_hbm, pg_hbm, sg, lg_hbm, gg,
+    out, pg, lg, out_sem, pv, hv, ogv, wa, ia, mbh, mbl, ibh, ibl, tr, ti,
     halo, ext, gext, kf, vf, qT, scT, G, pc, taps, sb, rb, F, bh, bl, SH, SU, SD, SP,
     nsb, nrb, ar1, ar1r, ar1s, ar1q, ar2, ar2r, ar2s, ar2q,
     in_sem, xs, xr, hs, hr, ns, nr, as_, ar_,
@@ -113,12 +115,24 @@
             src_ref=sb.at[k, rows16(t)], dst_ref=rb.at[k, rows16(me)],
             send_sem=xs.at[k], recv_sem=xr.at[k], device_id={"ctx": t}, device_id_type=MESH)
 
-    def exchange(k):
-        def one(i, _):
-            send_to(k, lax.rem(me + i, NP)).start()
-            return _
-
-        lax.fori_loop(1, NP, one, 0)
+    my_z = me // 16
+    my_half = lax.rem(me // 8, 2)
+
+    def exchange(k, fill):
+        def block(i, _):
+            z = jnp.bitwise_xor(my_z, 3 - i // 2)
+            half = jnp.where(lax.rem(i, 2) == 0, 1 - my_half, my_half)
+            b = 2 * z + half
+            fill(b, pl.ds(pl.multiple_of(b * 128, 128), 128))
+
+            def one(j, _):
+                send_to(k, b * 8 + lax.rem(me + j, 8)).start()
+                return _
+
+            lax.fori_loop(jnp.where(i == NB - 1, 1, 0), 8, one, 0)
+            return _
+
+        lax.fori_loop(0, NB, block, 0)
         pltpu.make_async_copy(sb.at[k, rows16(me)], rb.at[k, rows16(me)], xr.at[k]).start()
 
     def arrived(k):
@@ -130,11 +144,9 @@
 
     loads[0].wait()
 
-    def h_block(b, _):
-        sb[X_H, pl.ds(pl.multiple_of(b * 128, 128), 128), :] = hv[:, lanes(b)].T.astype(BF16)
-        return _
-
-    lax.fori_loop(0, NB, h_block, 0)
+    def h_block(b, R):
+        sb[X_H, R, :] = hv[:, lanes(b)].T.astype(BF16)
+
     loads[1].wait()
 
     pl.semaphore_wait(bar, NP - 1 + NH - 1)
@@ -145,7 +157,7 @@
         src_ref=pv.at[:, pl.ds(NT - 16, 16), :], dst_ref=halo, send_sem=hs.at[0], recv_sem=hr.at[0],
         device_id={"ctx": nxt}, device_id_type=MESH)
     halo_copy.start()
-    exchange(X_H)
+    exchange(X_H, h_block)
 
     member = (
         lax.broadcasted_iota(jnp.int32, (NG, NC), 1) // GROUP
@@ -158,12 +170,11 @@
     loads[2].wait()
 
     halo_copy.wait()
-    first = jnp.where(me == 0, 0.0, 1.0).astype(F32)
     for i in range(3):
         edge = halo[i].astype(F32)
         ext[i, pl.ds(0, 8), :] = jnp.where(me == 0, 0.0, edge[8:, :])
 
-    def feat_block(b, _):
+    def feat_block(b, R):
         L = lanes(b)
         f = []
         for i in range(3):
@@ -171,15 +182,12 @@
             for j in range(1, KS):
                 acc = acc + pc[i, pl.ds(j, 1), L] * ext[i, pl.ds(8 - j, NT), L]
             f.append(acc.astype(BF16).astype(F32))
-        R = pl.ds(pl.multiple_of(b * 128, 128), 128)
         sb[X_U, R, :] = (f[1] * f[2]).T.astype(BF16)
         kf[:, L] = f[1]
         vf[:, L] = f[2]
         qT[R, :] = f[0].T
-        return _
-
-    lax.fori_loop(0, NB, feat_block, 0)
-    exchange(X_U)
+
+    exchange(X_U, feat_block)
 
     def sc_block(b, _):
         L = lanes(b)
@@ -209,7 +217,7 @@
                 bl[R, :] = lo
             return _
 
-        lax.fori_loop(0, CH // 2, pair, 0)
+        lax.fori_loop(0, CH // 2, pair, 0, unroll=UNP)
 
         def block(r, _):
             R = pl.ds(pl.multiple_of(r * 256, 256), 256)
@@ -217,7 +225,7 @@
                 dot(bh[R, :], mbh[...]) + dot(bh[R, :], mbl[...]) + dot(bl[R, :], mbh[...]))
             return _
 
-        lax.fori_loop(0, NC // 256, block, 0)
+        lax.fori_loop(0, NC // 256, block, 0, unroll=UNB)
 
     def inverse(k, A, B, conj):
         def block(r, _):
@@ -234,7 +242,7 @@
             SP[R, :] = dot(hi, ibh[...]) + dot(hi, ibl[...]) + dot(lo, ibh[...])
             return _
 
-        lax.fori_loop(0, NC // 256, block, 0)
+        lax.fori_loop(0, NC // 256, block, 0, unroll=UNB)
 
         def pair(g, _):
             cols = []
@@ -250,15 +258,18 @@
                 F[pl.ds(2 * g + e, NP, stride=CH), :] = z[:, e * NT:(e + 1) * NT]
             return _
 
-        lax.fori_loop(0, CH // 2, pair, 0)
-        sb[k] = F[...].astype(BF16)
+        lax.fori_loop(0, CH // 2, pair, 0, unroll=UNP)
+
+        def fill(b, R):
+            sb[k, R, :] = F[R, :].astype(BF16)
+
+        exchange(k, fill)
 
     arrived(X_H)
     forward(X_H, SH)
     arrived(X_U)
     forward(X_U, SU)
     inverse(X_Z, SU, SH, False)
-    exchange(X_Z)
     arrived(X_Z)
 
     def gate_block(b, carry):
@@ -302,16 +313,13 @@
     inner = rs * tot[1:2] / D
     coef = rs * rs * inner
 
-    def d_block(b, _):
-        R = pl.ds(pl.multiple_of(b * 128, 128), 128)
+    def d_block(b, R):
         q = qT[R, :]
         g = G[R, :]
         grad = rs * scT[R, :] - coef * g
         sb[X_D, R, :] = (grad * q).astype(BF16)
-        return _
-
-    lax.fori_loop(0, NB, d_block, 0)
-    exchange(X_D)
+
+    exchange(X_D, d_block)
 
     def out_block(b, _):
         L = lanes(b)
@@ -332,6 +340,9 @@
             dst_ref=gext.at[pl.ds(lo, n), pl.ds(NT, 8), :],
             send_sem=hs.at[s], recv_sem=hr.at[s], device_id={"ctx": prv}, device_id_type=MESH)
 
+    stores = [pltpu.make_async_copy(out, out_hbm, out_sem.at[0])]
+    stores += [pltpu.make_async_copy(pg.at[i], pg_hbm.at[i], out_sem.at[1 + i]) for i in range(3)]
+    stores[0].start()
     edge0 = edge_copy(0, 1, 1)
     edge0.start()
 
@@ -362,6 +373,7 @@
             return _
 
         lax.fori_loop(0, NB, block, 0)
+        stores[1 + i].start()
 
     my_y = lax.rem(me // 2, 8)
     my_zc = (me // 16) * 2 + lax.rem(me, 2)
@@ -379,9 +391,7 @@
     arrived(X_D)
     forward(X_D, SD)
     inverse(X_DU, SH, SD, True)
-    exchange(X_DU)
     inverse(X_DH, SU, SD, True)
-    exchange(X_DH)
 
     ar1s[...] = group_wait(ar1r, ar_.at[0])
     group_sum(ar1s, ar1q, as_.at[1], ar_.at[1], my_zc, 8, zc_peer)
@@ -419,6 +429,8 @@
         return _
 
     lax.fori_loop(0, NB, filt_block, 0)
+    stores.append(pltpu.make_async_copy(lg, lg_hbm, out_sem.at[4]))
+    stores[4].start()
 
     a1 = group_wait(ar1q, ar_.at[1])
     gg[...] = a1[0:8]
@@ -427,6 +439,8 @@
     sg[1] = a2[0:KS, 0:NG]
     sg[2] = a2[0:KS, NG:]
 
+    for c in stores:
+        c.wait()
     for k in range(6):
         sent(k)
     group_sent(nrb, ns, NH)
@@ -434,6 +448,19 @@
     group_sent(ar1q, as_.at[1], 8)
     group_sent(ar2r, as_.at[2], 8)
     group_sent(ar2q, as_.at[3], 8)
+
+
+def hand_over(*refs):
+    ins, outs, bufs, sem = refs[:5], refs[5:10], refs[10:15], refs[15]
+    first = [pltpu.make_async_copy(a, b, sem.at[i]) for i, (a, b) in enumerate(zip(ins, bufs))]
+    last = [pltpu.make_async_copy(b, c, sem.at[5 + i]) for i, (b, c) in enumerate(zip(bufs, outs))]
+    for c in first:
+        c.start()
+    for a, c in zip(first, last):
+        a.wait()
+        c.start()
+    for c in last:
+        c.wait()
 
 
 def on_device(projections, grouped_short_filters, long_filter, norm_gain, out_grad):
@@ -451,8 +478,12 @@
             jax.ShapeDtypeStruct((8, 128), F32),
         ],
         in_specs=[anywhere, vmem, anywhere, vmem, anywhere] + [anywhere] * 8,
-        out_specs=[vmem] * 5,
+        out_specs=[anywhere, anywhere, vmem, anywhere, vmem],
         scratch_shapes=[
+            pltpu.VMEM((NT, NC), BF16),
+            pltpu.VMEM((3, NT, NC), BF16),
+            pltpu.VMEM((NT, NC), F32),
+            dma((5,)),
             pltpu.VMEM((3, NT, NC), BF16),
             pltpu.VMEM((NT, NC), F32),
             pltpu.VMEM((NT, NC), BF16),
@@ -489,7 +520,13 @@
             collective_id=0, has_side_effects=True, vmem_limit_bytes=56 * 2**20),
     )(projections, grouped_short_filters, long_filter, norm_gain.reshape(8, 128), out_grad,
       *[jnp.asarray(t) for t in tabs])
-    out, pg, sg, lg, gg = res
+    out, pg, sg, lg, gg = pl.pallas_call(
+        hand_over,
+        out_shape=[jax.ShapeDtypeStruct(r.shape, r.dtype) for r in res],
+        in_specs=[anywhere] * 5,
+        out_specs=[anywhere] * 5,
+        scratch_shapes=[*[pltpu.VMEM(r.shape, r.dtype) for r in res], dma((10,))],
+    )(*res)
     return out, pg, sg, lg, gg.reshape(NC)
 
 

time: 104 us -> 89.8 us (0.86)
  Pallas kernels: 97.1 us -> 88.9 us
  local copies, waits for them, and re-layouts: 5.79 us -> 0 us
    pallas_call x1, Pallas kernels: 97.1 us -> 86.5 us  [on_device(): pl.pallas_call(kernel, out_shape=[jax.ShapeDtypeStruct((NT, NC), BF16), j...]
    unnamed x11 -> x0, local copies, waits for them, and re-layouts: 5.79 us -> none
    pallas_call x0 -> x1, Pallas kernels: none -> 2.36 us  [on_device(): pl.pallas_call(hand_over, out_shape=[jax.ShapeDtypeStruct(r.shape, r.dtyp...]
where the time goes in v2:
time: 89.8 us; the launch traced here: 89.5 us
  Pallas kernels  88.9 us (99%)
    pallas_call x1, Pallas kernels, on_device(): pl.pallas_call(kernel, out_shape=[jax.ShapeDtypeStruct((NT, NC), BF16), j...  86.5 us
    pallas_call x1, Pallas kernels, on_device(): pl.pallas_call(hand_over, out_shape=[jax.ShapeDtypeStruct(r.shape, r.dtyp...  2.36 us

profile of v2, /device:TPU:1, one launch (start us, length us, event | category | flops | bytes accessed | tf_op | source)
XLA Modules:
  0.0 89.5 jit_solution(4443085712550146653)
XLA Ops:
  0.6 86.5 %shard_map.164 = (bf16[128,1024]{1,0:T(8,128)(2,1)}, bf16[3,128,1024]{2,1,0:T(8,128)(2,1)}, f32[3,7,64]{2,1,0:T(8,128)}, f32[128,1024]{1,0:T(8,128)}, f32[8,128]{1,0:T(8,128)}) custom-call(bf16[3,128,1024]{2,1,0:T(8,128)(2,1)} %proj_hbm.1, f32[3,7,64]{2,1,0:T(8,128)} %gsf.1, f32[128,1024]{1,0:T(8,128)} %h_hbm.1, f32[8,128]{1,0:T(8,128)} %bitcast.2, ...), custom_call_target="tpu_custom_call" | custom-call | tf_op jit(solution)/shard_map/pallas_call | solution.py:471
  87.2 2.4 %shard_map.165 = (bf16[128,1024]{1,0:T(8,128)(2,1)}, bf16[3,128,1024]{2,1,0:T(8,128)(2,1)}, f32[3,7,64]{2,1,0:T(8,128)}, f32[128,1024]{1,0:T(8,128)}, f32[8,128]{1,0:T(8,128)}) custom-call(bf16[128,1024]{1,0:T(8,128)(2,1)} %get-tuple-element.15.refs_0_, bf16[3,128,1024]{2,1,0:T(8,128)(2,1)} %get-tuple-element.16.refs_1_, ...), custom_call_target="tpu_custom_call" | custom-call | tf_op jit(solution)/shard_map/pallas_call | solution.py:523

commit v3 on v2

--- a/solution.py
+++ b/solution.py
@@ -24,7 +24,7 @@
 CH = NC // NP
 NB = NC // 128
 NG = NC // GROUP
-UNP = 4
+UNP = 8
 UNB = 4
 
 X_H, X_U, X_Z, X_D, X_DU, X_DH = range(6)
@@ -142,12 +142,19 @@
         part = sb.at[k, pl.ds(0, NC - CH)]
         pltpu.make_async_copy(part, part, xs.at[k]).wait()
 
+    member = (
+        lax.broadcasted_iota(jnp.int32, (NG, NC), 1) // GROUP
+        == lax.broadcasted_iota(jnp.int32, (NG, NC), 0)
+    ).astype(F32)
+    loads[1].wait()
+    for i in range(3):
+        pc[i, pl.ds(0, KS), :] = jnp.dot(
+            gsf[i], member, preferred_element_type=F32, precision=lax.Precision.HIGHEST)
+        ext[i, pl.ds(8, NT), :] = pv[i].astype(F32)
+
     loads[0].wait()
-
-    def h_block(b, R):
-        sb[X_H, R, :] = hv[:, lanes(b)].T.astype(BF16)
-
-    loads[1].wait()
+    for b in range(NB):
+        sb[X_H, pl.ds(b * 128, 128), :] = hv[:, pl.ds(b * 128, 128)].T.astype(BF16)
 
     pl.semaphore_wait(bar, NP - 1 + NH - 1)
 
@@ -157,17 +164,7 @@
         src_ref=pv.at[:, pl.ds(NT - 16, 16), :], dst_ref=halo, send_sem=hs.at[0], recv_sem=hr.at[0],
         device_id={"ctx": nxt}, device_id_type=MESH)
     halo_copy.start()
-    exchange(X_H, h_block)
-
-    member = (
-        lax.broadcasted_iota(jnp.int32, (NG, NC), 1) // GROUP
-        == lax.broadcasted_iota(jnp.int32, (NG, NC), 0)
-    ).astype(F32)
-    for i in range(3):
-        pc[i, pl.ds(0, KS), :] = jnp.dot(
-            gsf[i], member, preferred_element_type=F32, precision=lax.Precision.HIGHEST)
-        ext[i, pl.ds(8, NT), :] = pv[i].astype(F32)
-    loads[2].wait()
+    exchange(X_H, lambda b, R: None)
 
     halo_copy.wait()
     for i in range(3):
@@ -188,6 +185,8 @@
         qT[R, :] = f[0].T
 
     exchange(X_U, feat_block)
+
+    loads[2].wait()
 
     def sc_block(b, _):
         L = lanes(b)
@@ -356,7 +355,7 @@
             taps[i, pl.ds(KS, 1), L] = jnp.zeros((1, 128), F32)
             return _
 
-        lax.fori_loop(0, NB, block, 0)
+        lax.fori_loop(0, NB, block, 0, unroll=2)
         return lax.dot_general(
             taps[i], member, (((1,), (1,)), ((), ())), preferred_element_type=F32,
             precision=lax.Precision.HIGHEST)
@@ -408,7 +407,7 @@
         gext[2, pl.ds(0, NT), L] = m * kf[:, L]
         return _
 
-    lax.fori_loop(0, NB, mix_block, 0)
+    lax.fori_loop(0, NB, mix_block, 0, unroll=4)
     edge12 = edge_copy(1, 2, 2)
     edge12.start()
     t1 = taps_of(1)

time: 89.8 us -> 88.9 us (0.990)
  Pallas kernels: 88.9 us -> 88 us
where the time goes in v3:
time: 88.9 us; the launch traced here: 88.7 us
  Pallas kernels  88 us (99%)
    pallas_call x1, Pallas kernels, on_device(): pl.pallas_call(kernel, out_shape=[jax.ShapeDtypeStruct((NT, NC), BF16), j...  85.7 us
    pallas_call x1, Pallas kernels, on_device(): pl.pallas_call(hand_over, out_shape=[jax.ShapeDtypeStruct(r.shape, r.dtyp...  2.36 us

profile of v3, /device:TPU:1, one launch (start us, length us, event | category | flops | bytes accessed | tf_op | source)
XLA Modules:
  0.0 88.7 jit_solution(5617926608973398354)
XLA Ops:
  0.6 85.7 %shard_map.164 = (bf16[128,1024]{1,0:T(8,128)(2,1)}, bf16[3,128,1024]{2,1,0:T(8,128)(2,1)}, f32[3,7,64]{2,1,0:T(8,128)}, f32[128,1024]{1,0:T(8,128)}, f32[8,128]{1,0:T(8,128)}) custom-call(bf16[3,128,1024]{2,1,0:T(8,128)(2,1)} %proj_hbm.1, f32[3,7,64]{2,1,0:T(8,128)} %gsf.1, f32[128,1024]{1,0:T(8,128)} %h_hbm.1, f32[8,128]{1,0:T(8,128)} %bitcast.2, ...), custom_call_target="tpu_custom_call" | custom-call | tf_op jit(solution)/shard_map/pallas_call | solution.py:470
  86.3 2.4 %shard_map.165 = (bf16[128,1024]{1,0:T(8,128)(2,1)}, bf16[3,128,1024]{2,1,0:T(8,128)(2,1)}, f32[3,7,64]{2,1,0:T(8,128)}, f32[128,1024]{1,0:T(8,128)}, f32[8,128]{1,0:T(8,128)}) custom-call(bf16[128,1024]{1,0:T(8,128)(2,1)} %get-tuple-element.15.refs_0_, bf16[3,128,1024]{2,1,0:T(8,128)(2,1)} %get-tuple-element.16.refs_1_, ...), custom_call_target="tpu_custom_call" | custom-call | tf_op jit(solution)/shard_map/pallas_call | solution.py:522
